TPU v7x, 32 devices: a whole 2x2x4 slice. The times are simulated.
32 devices in a mesh: blk: 8 (over y, x, core), freq: 4 (over z).
Axes of the slice: x: 2, y: 2, z: 4, core: 2. Of those that a mesh axis runs over, the one named last changes fastest.
Arguments:
- raw_voltages: bfloat16 [512, 530432], P(('blk', 'freq')), may hold values from -6 to 6
- filter_taps: float32 [4, 2048], replicated, may hold values from -3 to 3
- input_order: int32 [512], P('blk'), may hold values from 0 to 511, as said below
- chan_order: int32 [1024], replicated, may hold values from 0 to 1023, each once
Outputs:
- visibilities: float32 [2, 5, 64, 512, 1024], P(None, None, None, 'blk', 'freq')
Inputs may be any that keep to these rules, and one draw needn't show every extreme that they name: input_order is a permutation, and slot k holds a raw input of the same aligned block of 64 slots as k. `chan_order`: each channel once.
All inputs are finite; a program needn't handle non-finite values.
Results may differ from a plain program's by a relative error of at most 0.0029.
Values may be sent and summed in bfloat16 or wider, within the bound.
A program may use at most 256 MiB of HBM per device.

v0:
```python
import math

import jax
import jax.numpy as jnp
from jax import lax
from jax.sharding import PartitionSpec as P

TAPS = 4
SPECTRA = 256


def from_partner(value, axis, distance):
    mask = 2**distance
    pairs = [(source, source ^ mask) for source in range(lax.axis_size(axis))]
    return lax.ppermute(value, axis, pairs)


def passed_along(value, axis, steps):
    count = lax.axis_size(axis)
    pairs = [(source, (source + steps) % count) for source in range(count)]
    return lax.ppermute(value, axis, pairs)


def make_table(chan_order):
    channel_count = chan_order.shape[0]
    sample_index = jnp.arange(2 * channel_count, dtype=jnp.int32)
    product = sample_index[:, None] * chan_order[None, :] % (2 * channel_count)
    phase_arg = product.astype(jnp.float32) * (math.pi / channel_count)
    return jnp.concatenate([jnp.cos(phase_arg), -jnp.sin(phase_arg)], axis=1) / math.sqrt(
        channel_count
    )


def filter_bank(raw_voltages, filter_taps, dft_table):
    input_count = raw_voltages.shape[0]
    channel_count = dft_table.shape[1] // 2
    frames = raw_voltages.astype(jnp.float32).reshape(
        input_count, SPECTRA + TAPS - 1, 2 * channel_count
    )
    filtered = filter_taps[0] * frames[:, 0:SPECTRA]
    for tap_index in range(1, TAPS):
        filtered = filtered + filter_taps[tap_index] * frames[:, tap_index : tap_index + SPECTRA]
    transformed = jnp.dot(
        filtered.reshape(input_count * SPECTRA, 2 * channel_count),
        dft_table,
        precision=lax.Precision.HIGHEST,
    )
    transformed = transformed.reshape(input_count, SPECTRA, 2, channel_count).transpose(0, 2, 1, 3)
    return transformed.astype(jnp.bfloat16)


def sectioned_turn(spectra_local):
    input_count, parts_count, spectra_count, channel_count = spectra_local.shape
    ranks = lax.axis_size("freq")
    block_width = channel_count // ranks
    current = spectra_local.reshape(input_count, parts_count, spectra_count, ranks, block_width)
    position = lax.axis_index("freq")
    for bit_level in range(ranks.bit_length() - 1):
        inputs_now = current.shape[0]
        groups = current.shape[3]
        split_view = current.reshape(
            inputs_now, parts_count, spectra_count, groups // 2, 2, block_width
        )
        my_bit = position >> bit_level & 1
        kept = lax.dynamic_index_in_dim(split_view, my_bit, 4, keepdims=False)
        outgoing = lax.dynamic_index_in_dim(split_view, 1 - my_bit, 4, keepdims=False)
        incoming = from_partner(outgoing, "freq", bit_level)
        lower = jnp.where(my_bit == 0, kept, incoming)
        upper = jnp.where(my_bit == 0, incoming, kept)
        current = jnp.concatenate([lower, upper], axis=0)
    return current.reshape(current.shape[0], parts_count, spectra_count, block_width)


def per_device(raw_voltages, filter_taps, input_order, chan_order):
    dft_table = make_table(chan_order)
    spectra_local = filter_bank(raw_voltages, filter_taps, dft_table)
    turned = sectioned_turn(spectra_local)
    tile_size = turned.shape[0]
    spectra_count = turned.shape[2]
    block_width = turned.shape[3]
    row_index = input_order - lax.axis_index("blk") * tile_size
    own_tile = jnp.take(turned, row_index, axis=0)
    plain = own_tile.reshape(tile_size, 2 * spectra_count, block_width)
    rotated = jnp.concatenate([own_tile[:, 1], -own_tile[:, 0]], axis=1)

    def correlate(partner):
        vis_real = (
            jnp.einsum("jtc,itc->jic", partner, plain, preferred_element_type=jnp.float32)
            / spectra_count
        )
        vis_imag = (
            jnp.einsum("jtc,itc->jic", partner, rotated, preferred_element_type=jnp.float32)
            / spectra_count
        )
        return jnp.stack([vis_real, vis_imag])

    half_loop = lax.axis_size("blk") // 2
    local_block = correlate(plain)

    def advance(carried, unused):
        arrived = passed_along(carried, "blk", 1)
        return (arrived, correlate(arrived))

    _, later_blocks = lax.scan(advance, plain, None, length=half_loop)
    stacked = jnp.concatenate([local_block[None], later_blocks], axis=0)
    return stacked.transpose(1, 0, 2, 3, 4)


def solution(mesh):
    placed = (P(("blk", "freq"), None), P(), P("blk"), P())
    return jax.shard_map(
        per_device,
        mesh=mesh,
        in_specs=placed,
        out_specs=P(None, None, None, "blk", "freq"),
        check_vma=False,
    )
```

profile of v0, /device:TPU:0, one launch (start us, length us, event | category | flops | bytes accessed | tf_op | source)
XLA Modules:
  0.0 2231.5 jit_solution(15726649395666974188)
XLA Ops:
  0.9 37.9 %fusion.23 = (f32[2048,1024]{0,1:T(8,128)}, f32[2048,1024]{0,1:T(8,128)}) fusion(s32[1024]{0:T(1024)} %param.9), kind=kLoop, calls=%fused_computation.53 | loop fusion | flops 31457280 | bytes 16781312 | tf_op jit(solution)/shard_map/cos | solution.py:29
  38.9 26.2 %reshape.36 = f32[16,259,2048]{2,1,0:T(8,128)} reshape(bf16[16,530432]{1,0:T(8,128)(2,1)} %param.6) | data formatting | bytes 50921472 | tf_op jit(solution)/shard_map/reshape | solution.py:37
  76.8 236.6 %convert_bitcast_fusion = bf16[16,2,256,1024]{3,2,1,0:T(8,128)(2,1)} fusion(f32[2,1024,2048,1]{2,1,0,3:T(8,128)} %bitcast.85, f32[16,259,2048]{2,1,0:T(8,128)} %reshape.36, f32[2048]{0:T(1024)S(1)} %bitcast.88, f32[2048]{0:T(1024)S(1)} %bitcast.89, f32[2048]{0:T(1024)S(1)} %bitcast.87, f32[2048]{0:T(1024)S(1)} %bitcast.86), kind=kOutput, calls=%fused_computation.24 | convolution fusion | flops 206225539072 | bytes 167804928 | tf_op jit(solution)/shard_map/dot_general | solution.py:43
  313.5 27.7 %reshape_reshape.3 = bf16[16,2,256,2,2,256]{5,4,3,2,1,0:T(2,128)(2,1)} reshape(bf16[16,2,256,1024]{3,2,1,0:T(8,128)(2,1)} %convert_bitcast_fusion) | data formatting | bytes 33554432 | tf_op jit(solution)/shard_map/reshape;reshape | solution.py:61
  341.2 37.9 %constant_dynamic-slice_fusion.1 = (bf16[16,2,256,2,1,256]{5,4,3,2,1,0:T(2,128)(2,1)}, bf16[16,2,256,2,1,256]{5,4,3,2,1,0:T(2,128)(2,1)S(1)}) fusion(bf16[16,2,256,2,2,256]{5,4,3,2,1,0:T(2,128)(2,1)} %reshape_reshape.3, s32[]{:T(128)S(6)} %select_n.61, s32[]{:T(128)S(6)} %select_n.62), kind=kLoop, calls=%fused_computation.58 | loop fusion | bytes 33554440 | tf_op jit(solution)/shard_map/jit(dynamic_index_in_dim)/dynamic_slice | solution.py:65
  386.5 180.8 %collective-permute-done.1 = bf16[16,2,256,2,256]{4,2,3,1,0:T(8,128)(2,1)} collective-permute-done((bf16[16,2,256,2,256]{4,2,3,1,0:T(8,128)(2,1)}, bf16[16,2,256,2,256]{4,2,3,1,0:T(8,128)(2,1)}, u32[]{:S(2)}, u32[]{:S(2)}) %collective-permute-start.1) | collective-permute-done | bytes 8388640 | tf_op jit(solution)/shard_map/ppermute | solution.py:15
  592.0 359.8 %collective-permute-done.2 = bf16[32,2,256,1,256]{4,2,3,1,0:T(8,128)(2,1)} collective-permute-done((bf16[32,2,256,1,256]{4,2,3,1,0:T(8,128)(2,1)}, bf16[32,2,256,1,256]{4,2,3,1,0:T(8,128)(2,1)}, u32[]{:S(2)}, u32[]{:S(2)}) %collective-permute-start.2) | collective-permute-done | bytes 8388640 | tf_op jit(solution)/shard_map/ppermute | solution.py:15
  980.9 22.9 %copy.11 = bf16[64,2,256,256]{2,0,3,1:T(8,128)(2,1)} copy(bf16[64,2,256,256]{3,2,1,0:T(8,128)(2,1)} %gather_fusion) | data formatting | bytes 33554432 | tf_op jit(solution)/shard_map/jit(_take)/gather | solution.py:82
  1018.1 23.4 %copy.9 = bf16[64,512,256]{1,0,2:T(8,128)(2,1)} copy(bf16[64,512,256]{2,1,0:T(8,128)(2,1)} %bitcast_select_fusion) | data formatting | bytes 33554432 | tf_op jit(solution)/shard_map/jit(_take)/select_n | solution.py:82
  1080.4 16.7 multiply_bitcast_fusion.3
  1097.2 16.4 copy.33
  1135.5 1066.7 %while.12 = (s32[]{:T(128)}, bf16[64,512,256]{1,0,2:T(8,128)(2,1)}, f32[4,2,64,64,256]{4,3,2,0,1:T(8,128)}, bf16[64,512,256]{1,0,2:T(8,128)(2,1)}, bf16[64,512,256]{1,0,2:T(8,128)(2,1)}, /*index=5*/s32[]{:T(128)}) while((s32[]{:T(128)}, bf16[64,512,256]{1,0,2:T(8,128)(2,1)}, f32[4,2,64,64,256]{4,3,2,0,1:T(8,128)}, ...), condition=%wide.region_1.2_spmd, body=%wide.region_0.1_spmd.sunk | while | flops 2151677952 | bytes 226492544 | solution.py:104
  1135.5 184.0 %collective-permute-done = bf16[64,512,256]{1,0,2:T(8,128)(2,1)} collective-permute-done((bf16[64,512,256]{1,0,2:T(8,128)(2,1)}, bf16[64,512,256]{1,0,2:T(8,128)(2,1)}, u32[]{:S(2)}, u32[]{:S(2)}) %collective-permute-start) | collective-permute-done | bytes 16777248 | tf_op jit(solution)/shard_map/while/body/eval_jaxpr/ppermute | solution.py:21
  1319.5 16.4 multiply_bitcast_fusion.7
  1335.9 16.4 multiply_bitcast_fusion.6
  1402.2 184.0 %collective-permute-done = bf16[64,512,256]{1,0,2:T(8,128)(2,1)} collective-permute-done((bf16[64,512,256]{1,0,2:T(8,128)(2,1)}, bf16[64,512,256]{1,0,2:T(8,128)(2,1)}, u32[]{:S(2)}, u32[]{:S(2)}) %collective-permute-start) | collective-permute-done | bytes 16777248 | tf_op jit(solution)/shard_map/while/body/eval_jaxpr/ppermute | solution.py:21
  1586.2 16.4 multiply_bitcast_fusion.7
  1669.0 184.0 %collective-permute-done = bf16[64,512,256]{1,0,2:T(8,128)(2,1)} collective-permute-done((bf16[64,512,256]{1,0,2:T(8,128)(2,1)}, bf16[64,512,256]{1,0,2:T(8,128)(2,1)}, u32[]{:S(2)}, u32[]{:S(2)}) %collective-permute-start) | collective-permute-done | bytes 16777248 | tf_op jit(solution)/shard_map/while/body/eval_jaxpr/ppermute | solution.py:21
  1852.9 16.4 multiply_bitcast_fusion.7
  1869.4 16.4 multiply_bitcast_fusion.6
  1935.6 184.0 %collective-permute-done = bf16[64,512,256]{1,0,2:T(8,128)(2,1)} collective-permute-done((bf16[64,512,256]{1,0,2:T(8,128)(2,1)}, bf16[64,512,256]{1,0,2:T(8,128)(2,1)}, u32[]{:S(2)}, u32[]{:S(2)}) %collective-permute-start) | collective-permute-done | bytes 16777248 | tf_op jit(solution)/shard_map/while/body/eval_jaxpr/ppermute | solution.py:21
  2119.6 16.4 multiply_bitcast_fusion.7
  2136.0 16.4 multiply_bitcast_fusion.6
  2202.3 28.8 %maximum_bitcast_fusion.1 = f32[2,5,64,64,256]{4,3,2,1,0:T(8,128)} fusion(f32[4,2,64,64,256]{4,3,2,0,1:T(8,128)} %get-tuple-element.32, f32[1,2,64,64,256]{4,3,2,0,1:T(8,128)} %copy.15), kind=kLoop, calls=%fused_computation.5 | loop fusion | flops 10485760 | bytes 83886080 | tf_op jit(solution)/shard_map/transpose | solution.py:106
  (51 shorter events, 365.0 us)
Async XLA Ops:
  383.4 183.8 %collective-permute-start.1 = (bf16[16,2,256,2,256]{4,2,3,1,0:T(8,128)(2,1)}, bf16[16,2,256,2,256]{4,2,3,1,0:T(8,128)(2,1)}, u32[]{:S(2)}, u32[]{:S(2)}) collective-permute-start(bf16[16,2,256,2,256]{4,2,3,1,0:T(8,128)(2,1)} %bitcast.70), channel_id=1, source_target_pairs={{0,1},{1,0},{2,3},{3,2},{4,5},{5,4},{6,7},{7,6},{8,9},{9,8},{10,11... | collective-permute-start | bytes 25165832 | tf_op jit(solution)/shard_map/ppermute | solution.py:15
  581.8 10.2 copy-start.4
  589.2 362.6 %collective-permute-start.2 = (bf16[32,2,256,1,256]{4,2,3,1,0:T(8,128)(2,1)}, bf16[32,2,256,1,256]{4,2,3,1,0:T(8,128)(2,1)}, u32[]{:S(2)}, u32[]{:S(2)}) collective-permute-start(bf16[32,2,256,1,256]{4,2,3,1,0:T(8,128)(2,1)} %fusion.17), channel_id=1, source_target_pairs={{0,2},{1,3},{2,0},{3,1},{4,6},{5,7},{6,4},{7,5},{8,10},{9,11},{10,... | collective-permute-start | bytes 25165832 | tf_op jit(solution)/shard_map/ppermute | solution.py:15
  1051.7 3.3 copy-start.1
  1051.7 6.1 copy-start.2
  1097.2 16.4 copy-start
  1097.2 16.4 copy-start.3
  1135.5 184.0 %collective-permute-start = (bf16[64,512,256]{1,0,2:T(8,128)(2,1)}, bf16[64,512,256]{1,0,2:T(8,128)(2,1)}, u32[]{:S(2)}, u32[]{:S(2)}) collective-permute-start(bf16[64,512,256]{1,0,2:T(8,128)(2,1)} %get-tuple-element.102), channel_id=1, source_target_pairs={{0,4},{4,8},{8,12},{12,16},{16,20},{20,24},{24,28},{28,0},{1,5},{5... | collective-permute-start | bytes 50331656 | tf_op jit(solution)/shard_map/while/body/eval_jaxpr/ppermute | solution.py:21
  1402.2 184.0 %collective-permute-start = (bf16[64,512,256]{1,0,2:T(8,128)(2,1)}, bf16[64,512,256]{1,0,2:T(8,128)(2,1)}, u32[]{:S(2)}, u32[]{:S(2)}) collective-permute-start(bf16[64,512,256]{1,0,2:T(8,128)(2,1)} %get-tuple-element.102), channel_id=1, source_target_pairs={{0,4},{4,8},{8,12},{12,16},{16,20},{20,24},{24,28},{28,0},{1,5},{5... | collective-permute-start | bytes 50331656 | tf_op jit(solution)/shard_map/while/body/eval_jaxpr/ppermute | solution.py:21
  1669.0 184.0 %collective-permute-start = (bf16[64,512,256]{1,0,2:T(8,128)(2,1)}, bf16[64,512,256]{1,0,2:T(8,128)(2,1)}, u32[]{:S(2)}, u32[]{:S(2)}) collective-permute-start(bf16[64,512,256]{1,0,2:T(8,128)(2,1)} %get-tuple-element.102), channel_id=1, source_target_pairs={{0,4},{4,8},{8,12},{12,16},{16,20},{20,24},{24,28},{28,0},{1,5},{5... | collective-permute-start | bytes 50331656 | tf_op jit(solution)/shard_map/while/body/eval_jaxpr/ppermute | solution.py:21
  1935.6 184.0 %collective-permute-start = (bf16[64,512,256]{1,0,2:T(8,128)(2,1)}, bf16[64,512,256]{1,0,2:T(8,128)(2,1)}, u32[]{:S(2)}, u32[]{:S(2)}) collective-permute-start(bf16[64,512,256]{1,0,2:T(8,128)(2,1)} %get-tuple-element.102), channel_id=1, source_target_pairs={{0,4},{4,8},{8,12},{12,16},{16,20},{20,24},{24,28},{28,0},{1,5},{5... | collective-permute-start | bytes 50331656 | tf_op jit(solution)/shard_map/while/body/eval_jaxpr/ppermute | solution.py:21
where the time goes:
time: 2240 us; the launch traced here: 2230 us
  waiting for transfers between devices  1280 us (57%)
  matrix products  400 us (18%)
  local copies, waits for them, and re-layouts  345 us (15%)
  other arithmetic  203 us (9%)
    ppermute x4, waiting for transfers between devices, passed_along(): return lax.ppermute(value, axis, pairs)  736 us
    ppermute x2, waiting for transfers between devices, from_partner(): return lax.ppermute(value, axis, pairs)  541 us
    dot_general x1, matrix products, filter_bank(): jnp.dot(filtered.reshape(input_count * SPECTRA, 2 * channel_count), dft_t...  237 us
    dynamic_update_slice x8, local copies, waits for them, and re-layouts, per_device(): _, later_blocks = lax.scan(advance, plain, None, length=half_loop)  93.4 us
    dot_general x5, matrix products, correlate(): jnp.einsum('jtc,itc->jic', partner, plain, preferred_element_type=jnp.flo...  82.5 us
    dot_general x5, matrix products, correlate(): jnp.einsum('jtc,itc->jic', partner, rotated, preferred_element_type=jnp.f...  81.3 us
    while x4, local copies, waits for them, and re-layouts  56.2 us
    broadcast_in_dim x5, other arithmetic, per_device(): _, later_blocks = lax.scan(advance, plain, None, length=half_loop)  50 us
  transfers between devices with their start and end apart: 6, of which 6 were waited for; matrix products, arithmetic and copies ran while one was open for 0% of the time, Pallas kernels for 0%

commit v1 on v0

v1 whole, which is shorter than its diff:
```python
import math

import jax
import jax.numpy as jnp
from jax import lax
from jax.sharding import PartitionSpec as P

TAPS = 4
SPECTRA = 256


def make_table(chan_rows, channel_count):
    sample_count = 2 * channel_count
    fine = 32

    def turn(samples):
        product = samples * chan_rows[..., None] % sample_count
        phase = product.astype(jnp.float32) * (math.pi / channel_count)
        return jnp.cos(phase), jnp.sin(phase)

    coarse_cos, coarse_sin = turn(jnp.arange(sample_count // fine, dtype=jnp.int32) * fine)
    fine_cos, fine_sin = turn(jnp.arange(fine, dtype=jnp.int32))
    coarse_cos, coarse_sin = coarse_cos[..., :, None], coarse_sin[..., :, None]
    fine_cos, fine_sin = fine_cos[..., None, :], fine_sin[..., None, :]
    scale = 1.0 / math.sqrt(channel_count)
    whole = chan_rows.shape + (sample_count,)
    real = ((coarse_cos * fine_cos - coarse_sin * fine_sin) * scale).reshape(whole)
    imag = ((coarse_sin * fine_cos + coarse_cos * fine_sin) * -scale).reshape(whole)
    return jnp.stack([real, imag], axis=1)


def per_device(raw_voltages, filter_taps, input_order, chan_order):
    blk, freq = lax.axis_size("blk"), lax.axis_size("freq")
    count = blk * freq
    held = raw_voltages.shape[0]
    channel_count = chan_order.shape[0]
    width = channel_count // count
    tile = input_order.shape[0]
    inputs = held * count
    offsets = blk // 2 + 1

    order = lax.all_gather(input_order, "blk", tiled=True)
    rows = chan_order.reshape(freq, blk, width).transpose(1, 0, 2).reshape(count, width)
    table = make_table(rows, channel_count)

    frames = raw_voltages.reshape(held, SPECTRA + TAPS - 1, 2 * channel_count)
    filtered = filter_taps[0] * frames[:, 0:SPECTRA].astype(jnp.float32)
    for tap in range(1, TAPS):
        filtered = filtered + filter_taps[tap] * frames[:, tap : tap + SPECTRA].astype(jnp.float32)
    spectra = jnp.einsum(
        "drkm,itm->drkit", table, filtered, precision=lax.Precision.HIGH
    ).astype(jnp.bfloat16)
    turned = lax.all_to_all(spectra, ("blk", "freq"), 0, 0, tiled=True)

    by_channel = turned.transpose(2, 1, 0, 3, 4).reshape(width, 2, inputs, SPECTRA)
    chosen = (order[:, None] == jnp.arange(inputs, dtype=jnp.int32)[None, :]).astype(jnp.bfloat16)
    chosen = jnp.broadcast_to(chosen, (width,) + chosen.shape)
    parts = [
        jnp.einsum(
            "kpi,kit->kpt", chosen, by_channel[:, part], preferred_element_type=jnp.float32
        ).astype(jnp.bfloat16)
        for part in range(2)
    ]
    plain = jnp.concatenate(parts, axis=2)
    rotated = jnp.concatenate([parts[1], -parts[0]], axis=2)
    around = jnp.concatenate([plain[:, inputs - (offsets - 1) * tile :], plain], axis=1)
    blocks = []
    for b in range(blk):
        own = slice(b * tile, (b + 1) * tile)
        both = jnp.concatenate([plain[:, own], rotated[:, own]], axis=1)
        partners = around[:, b * tile : (b + offsets) * tile]
        product = jnp.einsum("kpt,kit->kpi", partners, both, preferred_element_type=jnp.float32)
        blocks.append((product * (1.0 / SPECTRA)).astype(jnp.bfloat16))
    sent = jnp.stack(blocks)
    arrived = lax.all_to_all(sent, "blk", 0, 0, tiled=True)
    arrived = arrived.reshape(blk * width, offsets, tile, 2, tile)
    return jnp.flip(arrived, axis=1).transpose(3, 1, 2, 4, 0).astype(jnp.float32)


def solution(mesh):
    placed = (P(("blk", "freq"), None), P(), P("blk"), P())
    return jax.shard_map(
        per_device,
        mesh=mesh,
        in_specs=placed,
        out_specs=P(None, None, None, "blk", "freq"),
        check_vma=False,
    )
```

time: 2240 us -> 1290 us (0.58)
  waiting for transfers between devices: 1280 us -> 238 us
  blocking collectives: 0 us -> 358 us
  matrix products: 400 us -> 276 us
  local copies, waits for them, and re-layouts: 345 us -> 254 us
  other arithmetic: 203 us -> 128 us
    ppermute x6 -> x0, waiting for transfers between devices: 1280 us -> none  [the longest x4 736 us: passed_along(): return lax.ppermute(value, axis, pairs)]
    all_to_all x0 -> x1, waiting for transfers between devices: none -> 238 us  [per_device(): turned = lax.all_to_all(spectra, ('blk', 'freq'), 0, 0, tiled=True)]
    all_to_all x0 -> x1, blocking collectives: none -> 237 us  [per_device(): arrived = lax.all_to_all(sent, 'blk', 0, 0, tiled=True)]
    dot_general x11, matrix products: 400 us -> 276 us  [the longest x1 135 us: per_device(): jnp.einsum('drkm,itm->drkit', table, filtered, precision=lax.Precision.HIGH)]
    unnamed x0 -> x1, blocking collectives: none -> 121 us
    convert_element_type x0 -> x1, local copies, waits for them, and re-layouts: none -> 95.9 us  [per_device(): jnp.flip(arrived, axis=1).transpose(3, 1, 2, 4, 0).astype(jnp.float32)]
    dynamic_update_slice x8 -> x0, local copies, waits for them, and re-layouts: 93.4 us -> none  [per_device(): _, later_blocks = lax.scan(advance, plain, None, length=half_loop)]
    reshape x1 -> x3, local copies, waits for them, and re-layouts: 26.2 us -> 89.3 us  [the longest x1 67.2 us: per_device(): arrived = arrived.reshape(blk * width, offsets, tile, 2, tile)]
  transfers between devices with their start and end apart: 6 -> 1, of which waited for: 6 -> 1; matrix products, arithmetic and copies ran while one was open for 0% -> 0% of each run, Pallas kernels for 0% -> 0%
where the time goes in v1:
time: 1290 us; the launch traced here: 1260 us
  blocking collectives  358 us (28%)
  matrix products  276 us (21%)
  local copies, waits for them, and re-layouts  254 us (20%)
  waiting for transfers between devices  238 us (18%)
  other arithmetic  128 us (10%)
    all_to_all x1, waiting for transfers between devices, per_device(): turned = lax.all_to_all(spectra, ('blk', 'freq'), 0, 0, tiled=True)  238 us
    all_to_all x1, blocking collectives, per_device(): arrived = lax.all_to_all(sent, 'blk', 0, 0, tiled=True)  237 us
    dot_general x1, matrix products, per_device(): jnp.einsum('drkm,itm->drkit', table, filtered, precision=lax.Precision.HIGH)  135 us
    unnamed x1, blocking collectives  121 us
    dot_general x8, matrix products, per_device(): jnp.einsum('kpt,kit->kpi', partners, both, preferred_element_type=jnp.flo...  115 us
    convert_element_type x1, local copies, waits for them, and re-layouts, per_device(): jnp.flip(arrived, axis=1).transpose(3, 1, 2, 4, 0).astype(jnp.float32)  95.9 us
    reshape x1, local copies, waits for them, and re-layouts, per_device(): arrived = arrived.reshape(blk * width, offsets, tile, 2, tile)  67.2 us
    convert_element_type x1, other arithmetic, per_device(): jnp.flip(arrived, axis=1).transpose(3, 1, 2, 4, 0).astype(jnp.float32)  42.3 us
  transfers between devices with their start and end apart: 1, of which 1 were waited for; matrix products, arithmetic and copies ran while one was open for 0% of the time, Pallas kernels for 0%

profile of v1, /device:TPU:0, one launch (start us, length us, event | category | flops | bytes accessed | tf_op | source)
XLA Modules:
  0.0 1262.4 jit_solution(4002019537004420744)
XLA Ops:
  5.9 21.3 %reshape.164 = bf16[16,259,2048]{2,1,0:T(8,128)(2,1)} reshape(bf16[16,530432]{1,0:T(8,128)(2,1)} %param.4) | data formatting | bytes 33947648 | tf_op jit(solution)/shard_map/reshape | solution.py:46
  27.2 21.6 %subtract_multiply_fusion = (f32[32,32,64,32]{3,2,1,0:T(8,128)}, f32[32,32,64,32]{3,2,1,0:T(8,128)}) fusion(f32[32,32,32]{2,1,0:T(8,128)S(1)} %get-tuple-element.28, f32[32,32,64]{2,1,0:T(8,128)S(1)} %get-tuple-element.26, f32[32,32,32]{2,1,0:T(8,128)S(1)} %get-tuple-element.27, f32[32,32,64]{2,1,0:T(8,128)S(1)} %get-tuple-element.25), kind=kLoop, calls=%fused_computation.39 | loop fusion | flops 16777216 | bytes 17563648 | tf_op jit(solution)/shard_map/mul | solution.py:27
  48.8 25.3 %mul.271 = f32[32,1,32,2048]{3,2,0,1:T(8,128)} reshape(f32[32,32,64,32]{3,2,1,0:T(8,128)} %get-tuple-element.19) | data formatting | bytes 16777216 | tf_op jit(solution)/shard_map/mul | solution.py:27
  74.1 25.3 %mul.276 = f32[32,1,32,2048]{3,2,0,1:T(8,128)} reshape(f32[32,32,64,32]{3,2,1,0:T(8,128)} %get-tuple-element.20) | data formatting | bytes 16777216 | tf_op jit(solution)/shard_map/mul | solution.py:28
  99.5 135.1 %fusion.43 = bf16[32,2,32,16,256]{4,2,3,1,0:T(8,128)(2,1)} fusion(bf16[16,259,2048]{2,1,0:T(8,128)(2,1)} %reshape.164, f32[2048]{0:T(1024)S(1)} %bitcast.96, f32[2048]{0:T(1024)S(1)} %bitcast.97, f32[2048]{0:T(1024)S(1)} %bitcast.95, f32[2048]{0:T(1024)S(1)} %bitcast.94, f32[32,1,32,2048]{3,2,1,0:T(8,128)} %bitcast.90, f32[32,1,32,2048]{3,2,1,0:T(8,128)} %bitcast.89), kind=kOutput, calls=%fused_computation.82 | convolution fusion | flops 103184072704 | bytes 100696064 | tf_op jit(solution)/shard_map/drkm,itm->drkit/dot_general | solution.py:50
  243.6 120.8 %all-reduce = s32[512]{0:T(512)S(1)} all-reduce(s32[512]{0:T(512)S(1)} %dynamic-update-slice), channel_id=1, replica_groups=mesh['blk'=8,'freq'=4] {'blk'}, use_global_device_ids=true, to_apply=%add | all-reduce | flops 512 | bytes 4096
  364.5 237.7 %all-to-all-done = bf16[32,2,32,16,256]{4,2,3,1,0:T(8,128)(2,1)} async-done(((bf16[32,2,32,16,256]{4,2,3,1,0:T(8,128)(2,1)}), bf16[32,2,32,16,256]{4,2,3,1,0:T(8,128)(2,1)}, u32[]{:S(2)}, u32[]{:S(2)}) %all-to-all-start) | async-done | bytes 16777248 | tf_op jit(solution)/shard_map/all_to_all | solution.py:53
  602.2 16.0 %copy.47 = bf16[32,2,32,16,256]{4,3,2,1,0:T(8,128)(2,1)} copy(bf16[32,2,32,16,256]{4,0,3,1,2:T(8,128)(2,1)} %bitcast.13) | data formatting | bytes 33554432 | tf_op jit(solution)/shard_map/transpose | solution.py:55
  625.3 18.7 %fusion.176 = (bf16[32,512,256]{1,2,0:T(8,128)(2,1)}, bf16[32,512,256]{1,2,0:T(8,128)(2,1)}) fusion(bf16[32,2,512,256]{3,2,1,0:T(8,128)(2,1)} %bitcast.88, bf16[512,512]{1,0:T(8,128)(2,1)S(1)} %fusion.151), kind=kOutput, calls=%fused_computation.197 | convolution fusion | flops 4303355904 | bytes 25690112 | tf_op jit(solution)/shard_map/kpi,kit->kpt/dot_general | solution.py:59
  650.1 17.6 %fusion.76 = (bf16[32,64,512]{1,2,0:T(8,128)(2,1)}, bf16[32,64,512]{1,2,0:T(8,128)(2,1)}, bf16[32,64,512]{1,2,0:T(8,128)(2,1)}, bf16[32,64,512]{1,2,0:T(8,128)(2...) fusion(bf16[32,512,256]{1,2,0:T(8,128)(2,1)} %get-tuple-element.30, ...), kind=kLoop, calls=%fused_computation.118 | loop fusion | flops 29360128 | bytes 31457280 | tf_op jit(solution)/shard_map/concatenate | solution.py:64
  667.6 17.4 %maximum_maximum_fusion = bf16[32,768,512]{1,2,0:T(8,128)(2,1)} fusion(bf16[32,512,256]{1,2,0:T(8,128)(2,1)} %copy-done, bf16[32,512,256]{1,2,0:T(8,128)(2,1)} %get-tuple-element.30, bf16[32,256,512]{1,2,0:T(8,128)(2,1)} %fusion.46), kind=kLoop, calls=%fused_computation.54 | loop fusion | flops 75497472 | bytes 50331648 | tf_op jit(solution)/shard_map/concatenate | solution.py:66
  685.1 19.1 %fusion.63 = (bf16[32,64,512]{1,2,0:T(8,128)(2,1)}, bf16[32,64,512]{1,2,0:T(8,128)(2,1)}, bf16[32,64,512]{1,2,0:T(8,128)(2,1)}, bf16[32,64,512]{1,2,0:T(8,128)(2...) fusion(bf16[32,512,256]{1,2,0:T(8,128)(2,1)} %copy-done, ...), kind=kLoop, calls=%fused_computation.105 | loop fusion | flops 29360128 | bytes 31457280 | tf_op jit(solution)/shard_map/concatenate | solution.py:65
  704.2 9.6 fusion.103
  713.8 17.5 %fusion.105 = bf16[8,32,320,128]{3,2,1,0:T(8,128)(2,1)} fusion(bf16[8,32,320,128]{3,2,1,0:T(8,128)(2,1)} %fusion.103, bf16[32,64,512]{1,2,0:T(8,128)(2,1)} %get-tuple-element.17, bf16[32,64,512]{1,2,0:T(8,128)(2,1)S(1)} %copy-done.1, bf16[32,768,512]{1,2,0:T(8,128)(2,1)} %maximum_maximum_fusion), kind=kOutput, calls=%fused_computation.148 | convolution fusion | flops 1353187328 | bytes 21495808 | tf_op jit(solution)/shard_map/kpt,kit->kpi/dot_general | solution.py:72
  731.2 11.0 fusion.107
  742.2 17.6 %fusion.109 = bf16[8,32,320,128]{3,2,1,0:T(8,128)(2,1)} fusion(bf16[8,32,320,128]{3,2,1,0:T(8,128)(2,1)} %fusion.107, bf16[32,64,512]{1,2,0:T(8,128)(2,1)} %get-tuple-element.14, bf16[32,64,512]{1,2,0:T(8,128)(2,1)} %get-tuple-element.9, bf16[32,768,512]{1,2,0:T(8,128)(2,1)} %maximum_maximum_fusion), kind=kOutput, calls=%fused_computation.152 | convolution fusion | flops 1353187328 | bytes 23592960 | tf_op jit(solution)/shard_map/kpt,kit->kpi/dot_general | solution.py:72
  759.8 10.0 fusion.111
  769.8 19.0 %fusion.113 = bf16[8,32,320,128]{3,2,1,0:T(8,128)(2,1)} fusion(bf16[8,32,320,128]{3,2,1,0:T(8,128)(2,1)} %fusion.111, bf16[32,64,512]{1,2,0:T(8,128)(2,1)} %get-tuple-element.16, bf16[32,64,512]{1,2,0:T(8,128)(2,1)} %get-tuple-element.11, bf16[32,512,256]{1,2,0:T(8,128)(2,1)} %get-tuple-element.30, bf16[32,512,256]{1,2,0:T(8,128)(2,1)} %copy-done), kind=kOutput, calls=%fused_computation.156 | convolution fusion | flops 1374158848 | bytes 27787264 | tf_op jit(solution)/shard_map/kpt,kit->kpi/dot_general | solution.py:72
  788.8 11.1 fusion.115
  799.8 19.4 %fusion.117 = bf16[8,32,320,128]{3,2,1,0:T(8,128)(2,1)} fusion(bf16[8,32,320,128]{3,2,1,0:T(8,128)(2,1)} %fusion.115, bf16[32,512,256]{1,2,0:T(8,128)(2,1)} %get-tuple-element.29, bf16[32,512,256]{1,2,0:T(8,128)(2,1)} %copy-done, bf16[32,512,256]{1,2,0:T(8,128)(2,1)} %get-tuple-element.30), kind=kOutput, calls=%fused_computation.160 | convolution fusion | flops 1388838912 | bytes 44564480 | tf_op jit(solution)/shard_map/kpt,kit->kpi/dot_general | solution.py:72
  819.2 237.4 %all_to_all.10 = bf16[8,32,320,128]{3,2,1,0:T(8,128)(2,1)} all-to-all(bf16[8,32,320,128]{3,2,1,0:T(8,128)(2,1)} %fusion.117), channel_id=1, replica_groups=mesh['blk'=8,'freq'=4] {'blk'}, dimensions={0} | all-to-all | bytes 41943040 | tf_op jit(solution)/shard_map/all_to_all | solution.py:75
  1056.6 67.2 %reshape.166 = bf16[256,5,64,2,64]{4,3,2,1,0:T(2,128)(2,1)} reshape(bf16[8,32,320,128]{3,2,1,0:T(8,128)(2,1)} %all_to_all.10) | data formatting | bytes 41943040 | tf_op jit(solution)/shard_map/reshape | solution.py:76
  1123.9 42.3 %convert_bitcast_fusion = f32[2,5,64,64,256]{3,0,2,1,4:T(2,128)} fusion(bf16[256,5,64,2,64]{4,3,2,1,0:T(2,128)(2,1)} %reshape.166), kind=kLoop, calls=%fused_computation | loop fusion | flops 10485760 | bytes 62914560 | tf_op jit(solution)/shard_map/convert_element_type | solution.py:77
  1166.1 95.9 %copy.66 = f32[2,5,64,64,256]{4,3,2,1,0:T(8,128)} copy(f32[2,5,64,64,256]{3,0,2,1,4:T(2,128)} %convert_bitcast_fusion) | data formatting | bytes 83886080 | tf_op jit(solution)/shard_map/convert_element_type | solution.py:77
  (28 shorter events, 27.5 us)
Async XLA Ops:
  234.6 7.4 copy-start.4
  234.6 8.7 copy-start.3
  234.6 367.6 %all-to-all-start = ((bf16[32,2,32,16,256]{4,2,3,1,0:T(8,128)(2,1)}), bf16[32,2,32,16,256]{4,2,3,1,0:T(8,128)(2,1)}, u32[]{:S(2)}, u32[]{:S(2)}) async-start(bf16[32,2,32,16,256]{4,2,3,1,0:T(8,128)(2,1)} %fusion.43), calls=%async_computation | async-start | bytes 33554432 | tf_op jit(solution)/shard_map/all_to_all | solution.py:53
  625.3 24.8 %copy-start = (bf16[32,512,256]{1,2,0:T(8,128)(2,1)}, bf16[32,512,256]{1,2,0:T(8,128)(2,1)S(1)}, u32[]{:S(2)}) copy-start(bf16[32,512,256]{1,2,0:T(8,128)(2,1)S(1)} %fusion.56) | copy-start | bytes 25165828
  685.1 19.1 %copy-start.2 = (bf16[32,64,512]{1,2,0:T(8,128)(2,1)S(1)}, bf16[32,64,512]{1,2,0:T(8,128)(2,1)}, u32[]{:S(2)}) copy-start(bf16[32,64,512]{1,2,0:T(8,128)(2,1)} %get-tuple-element.6) | copy-start | bytes 6291460
  704.2 9.6 copy-start.1
  713.8 46.0 %slice-start = ((s8[8388608]{0:T(1024)(128)(4,1)}), s8[4194304]{0:T(1024)(128)(4,1)S(1)}, s32[]{:S(2)}) async-start(s8[8388608]{0:T(1024)(128)(4,1)} %bitcast.85), calls=%async_computation.2 | async-start | bytes 8388608
  731.2 28.5 %slice-start.1 = ((s8[8388608]{0:T(1024)(128)(4,1)}), s8[4194304]{0:T(1024)(128)(4,1)S(1)}, s32[]{:S(2)}) async-start(s8[8388608]{0:T(1024)(128)(4,1)} %bitcast.85), calls=%async_computation.3 | async-start | bytes 8388608
